TPU v7x, 32 devices: a whole 2x2x4 slice. The times are simulated.
32 devices in a mesh: grp: 2 (over y), chan: 4 (over z), bl: 2 (over x), dir: 2 (over core).
Axes of the slice: x: 2, y: 2, z: 4, core: 2. Of those that a mesh axis runs over, the one named last changes fastest.
Arguments:
- visibility: bfloat16 [2, 8, 64, 4096], P(None, ('grp', 'chan'), 'bl'), parts along dimension 1, may hold values from -18 to 18
- coherency: bfloat16 [2, 8, 10, 64, 4096], P(None, ('grp', 'chan'), 'dir', 'bl'), parts along dimension 1, may hold values from -6 to 6
- gain_start: float32 [2, 8, 10, 512], P(None, ('grp', 'chan'), 'dir', 'bl'), parts along dimension 1, may hold values from -6 to 6
- dual_start: float32 [2, 8, 10, 512], P(None, ('grp', 'chan'), 'dir', 'bl'), parts along dimension 1, may hold values from -2 to 2
- penalty: float32 [20], P(('grp', 'dir')), parts along dimension 0, may hold values from 30 to 300
- tile_pairs: int32 [128, 2], P(('grp', 'bl')), parts along dimension 0, may hold values from 0 to 7, as said below
- valid_counts: int32 [128], P(('grp', 'bl')), parts along dimension 0, may hold values from 1024 to 4096, as said below
- station_order: int32 [1024], P('grp'), parts along dimension 0, may hold values from 0 to 511, each once
Outputs:
- gain_final: float32 [2, 8, 10, 512], P(None, ('grp', 'chan'), 'dir', 'bl'), parts along dimension 1
- dual_final: float32 [2, 8, 10, 512], P(None, ('grp', 'chan'), 'dir', 'bl'), parts along dimension 1
There are 2 independent parts, one for each index of `grp`. A program takes and returns all parts, laid end to end along the dimension named above; each array names one. Nothing has to cross between parts.
Inputs may be any that keep to these rules, and one draw needn't show every extreme that they name: `tile_pairs`: every ordered pair of tiles is the pair of exactly one block. `valid_counts`: some block has all slots valid.
All inputs are finite; a program needn't handle non-finite values.
Results may differ from a plain program's by a relative error of at most 0.0003.
Values may be sent and summed in bfloat16 or wider, within the bound.
A program may use at most 128 MiB of HBM per device.

v0:
```python
import functools

import jax
import jax.numpy as jnp
import numpy as np
from jax import lax
from jax.experimental import pallas as pl
from jax.experimental.pallas import tpu as pltpu
from jax.sharding import PartitionSpec as P

TILE = 64
NPOLY = 3
ITERS = 2
LANES = 128
PAD = 8
MESH = pl.DeviceIdType.MESH
F32 = jnp.float32
BF16 = jnp.bfloat16


def poly_coefficients(channels):
    points = (2.0 * np.arange(channels) + 1.0) / channels - 1.0
    powers = np.stack([points**d for d in range(NPOLY)], axis=1)
    columns = []
    for degree in range(NPOLY):
        own = np.zeros(NPOLY)
        own[degree] = 1.0
        column = powers[:, degree]
        for earlier, earlier_own in columns:
            dot = np.sum(earlier * column)
            column = column - dot * earlier
            own = own - dot * earlier_own
        norm = np.sqrt(np.sum(column * column))
        columns.append((column / norm, own / norm))
    return [[float(c) for c in own] for _, own in columns]


def basis_at(index, channels, coefficients):
    x = (2 * index + 1).astype(F32) * (1.0 / channels) - 1.0
    return [own[0] + x * (own[1] + x * own[2]) for own in coefficients]


def iota(shape, dim):
    return lax.broadcasted_iota(jnp.int32, shape, dim)


def onehot(mask):
    return jnp.where(mask, 1.0, 0.0).astype(BF16)


def two_pieces(values):
    high = values.astype(BF16)
    low = (values - high.astype(F32)).astype(BF16)
    return high, low


def kernel(
    nchan, nbl, ndir, coefficients,
    coh_hbm, vis_hbm, gain_ref, dual_ref, pen_ref, pairs_ref, cnt_ref, ord_ref,
    gout_ref, dout_ref,
    cohv, visv, gbuf, cbuf, psend, prec, dualp, natscr, dmat, emat, rmat, imat, amask,
    colg, rsplit, rowexp, tbuf, rowtile, coltile, limit,
    lsem, hsend, hrecv, gsend, grecv, csend, crecv, psems, precv,
):
    chan = lax.axis_index("chan")
    mb = lax.axis_index("bl")
    md = lax.axis_index("dir")
    mine = mb * ndir + md
    nown = nbl * ndir
    kl = gain_ref.shape[2]
    n = gain_ref.shape[3]
    stations = nbl * n
    nb = pairs_ref.shape[0]
    slots = TILE * TILE
    half = slots // ndir
    rows_half = half // TILE
    ntile = stations // TILE
    kall = ndir * kl

    def group_peer(offset):
        peer = lax.rem(mine + offset, nown)
        return lax.div(peer, ndir), lax.rem(peer, ndir)

    def chan_peer(offset):
        return lax.rem(chan + offset, nchan)

    def own_half():
        return pl.ds(pl.multiple_of(md * half, half), half)

    local = [
        pltpu.make_async_copy(coh_hbm.at[:, 0, :, :, own_half()], cohv.at[md], lsem.at[0]),
        pltpu.make_async_copy(vis_hbm.at[:, 0, :, own_half()], visv, lsem.at[1]),
    ]
    for copy in local:
        copy.start()

    barrier = pltpu.get_barrier_semaphore()
    for offset in range(1, nown):
        pb, pd = group_peer(offset)
        pl.semaphore_signal(barrier, inc=1, device_id={"bl": pb, "dir": pd}, device_id_type=MESH)
    for offset in range(1, nchan):
        pl.semaphore_signal(
            barrier, inc=1, device_id={"chan": chan_peer(offset)}, device_id_type=MESH
        )

    gbuf[0, mb, md] = jnp.zeros((2, PAD, n), F32)
    dualp[...] = jnp.zeros((2, PAD, n), F32)
    psend[...] = jnp.zeros(psend.shape, F32)
    for c in range(2):
        gbuf[0, mb, md, c, 0:kl, :] = gain_ref[c, 0]
        dualp[c, 0:kl, :] = dual_ref[c, 0]
    gain_now = gbuf[0, mb, md]
    dual_now = dualp[...]
    cbuf[0, chan] = gain_now + dual_now

    pl.semaphore_wait(barrier, nown - 1 + nchan - 1)

    halves = []
    for offset in range(1, ndir):
        peer = lax.rem(md + offset, ndir)
        source = lax.rem(md + ndir - offset, ndir)
        copy = pltpu.make_async_remote_copy(
            src_ref=coh_hbm.at[:, 0, :, :, pl.ds(pl.multiple_of(peer * half, half), half)],
            dst_ref=cohv.at[md],
            send_sem=hsend.at[offset],
            recv_sem=hrecv.at[md],
            device_id={"dir": peer},
            device_id_type=MESH,
        )
        arrival = pltpu.make_async_remote_copy(
            src_ref=coh_hbm.at[:, 0, :, :, pl.ds(pl.multiple_of(peer * half, half), half)],
            dst_ref=cohv.at[source],
            send_sem=hsend.at[offset],
            recv_sem=hrecv.at[source],
            device_id={"dir": peer},
            device_id_type=MESH,
        )
        halves.append((copy, arrival))

    def group_copies(source_of, target, send_sem, recv_sem, phase):
        made = []
        for offset in range(1, nown):
            pb, pd = group_peer(offset)
            sb, sd = group_peer(nown - offset)
            common = dict(
                src_ref=source_of(pb, pd),
                send_sem=send_sem.at[phase, offset],
                device_id={"bl": pb, "dir": pd},
                device_id_type=MESH,
            )
            copy = pltpu.make_async_remote_copy(
                dst_ref=target.at[phase, mb, md], recv_sem=recv_sem.at[phase, mine], **common
            )
            arrival = pltpu.make_async_remote_copy(
                dst_ref=target.at[phase, sb, sd],
                recv_sem=recv_sem.at[phase, sb * ndir + sd],
                **common,
            )
            made.append((copy, arrival))
        return made

    def gain_copies(phase):
        return group_copies(lambda pb, pd: gbuf.at[phase, mb, md], gbuf, gsend, grecv, phase)

    def term_copies(phase):
        return group_copies(lambda pb, pd: psend.at[phase, pb, pd], prec, psems, precv, phase)

    def chan_copies(phase):
        made = []
        for offset in range(1, nchan):
            peer = chan_peer(offset)
            source = chan_peer(nchan - offset)
            common = dict(
                src_ref=cbuf.at[phase, chan],
                send_sem=csend.at[phase, offset],
                device_id={"chan": peer},
                device_id_type=MESH,
            )
            copy = pltpu.make_async_remote_copy(
                dst_ref=cbuf.at[phase, chan], recv_sem=crecv.at[phase, chan], **common
            )
            arrival = pltpu.make_async_remote_copy(
                dst_ref=cbuf.at[phase, source], recv_sem=crecv.at[phase, source], **common
            )
            made.append((copy, arrival))
        return made

    def start(copies):
        for copy, _ in copies:
            copy.start()

    def arrive(copies):
        for _, arrival in copies:
            arrival.wait_recv()

    def finish(copies):
        for copy, _ in copies:
            copy.wait_send()

    everything = []
    gains = gain_copies(0)
    start(gains)
    start(halves)
    sums = chan_copies(0)
    start(sums)
    everything += [gains, halves, sums]

    order = ord_ref[...]
    wide = iota((ntile * LANES, stations), 0)
    dmat[...] = onehot(jnp.bitwise_and(wide, TILE - 1) + (wide // LANES) * TILE == order)
    shape = (2 * LANES, half)
    emat[...] = onehot(
        jnp.bitwise_and(iota(shape, 0), LANES - 1) == md * rows_half + iota(shape, 1) // TILE
    )
    shape = (2 * half, LANES)
    rmat[...] = onehot(jnp.bitwise_and(iota(shape, 0), half - 1) // TILE == iota(shape, 1))
    row_in = jnp.bitwise_and(iota((2 * LANES, stations), 0), LANES - 1)
    imat[...] = onehot(
        (row_in < rows_half) & (row_in + md * rows_half == jnp.bitwise_and(order, TILE - 1))
    )
    amask[...] = jnp.where(order // TILE == pairs_ref[:, 0:1], 1.0, 0.0)
    rowtile[...] = jnp.broadcast_to(pairs_ref[:, 0:1], (nb, LANES))
    coltile[...] = jnp.broadcast_to(pairs_ref[:, 1:2], (nb, LANES))
    square = jnp.where(
        iota((nb, nb), 0) == iota((nb, nb), 1), cnt_ref[...].astype(F32), 0.0
    )
    limit[...] = jnp.broadcast_to(jnp.sum(square, axis=1, keepdims=True), (nb, LANES))

    row_k = iota((PAD, n), 0)
    stiffness = jnp.ones((PAD, n), F32)
    for k in range(kl):
        stiffness = jnp.where(row_k == k, pen_ref[k], stiffness)

    def spread_gains(phase):
        held = jnp.concatenate(
            [
                jnp.concatenate([gbuf[phase, b, d, c] for b in range(nbl)], axis=1)
                for d in range(ndir)
                for c in range(2)
            ],
            axis=0,
        )
        first = held.astype(BF16)
        rest = held - first.astype(F32)
        second = rest.astype(BF16)
        third = (rest - second.astype(F32)).astype(BF16)
        pieces = jnp.concatenate([first, second, third], axis=0)
        found = lax.dot_general(
            pieces, dmat[...], (((1,), (1,)), ((), ())), preferred_element_type=F32
        )
        count = held.shape[0]
        natscr[...] = found[0:count] + found[count : 2 * count] + found[2 * count : 3 * count]

        def one(index, carry):
            group = index // kl
            row = group * PAD + lax.rem(index, kl)
            values = natscr[pl.ds(row, 1), :]
            by_row = jnp.zeros((nb, LANES), F32)
            by_col = jnp.zeros((nb, LANES), F32)
            for t in range(ntile):
                tile = values[:, t * LANES : (t + 1) * LANES]
                by_row = jnp.where(rowtile[...] == t, tile, by_row)
                by_col = jnp.where(coltile[...] == t, tile, by_col)
            colg[index] = by_col
            high, low = two_pieces(by_row)
            at = pl.ds(pl.multiple_of(index * nb, nb), nb)
            rsplit[at, 0:LANES] = high
            rsplit[at, LANES : 2 * LANES] = low
            return carry

        lax.fori_loop(0, 2 * kall, one, 0)

        def expand(step, carry):
            at = pl.ds(pl.multiple_of(step * 2 * LANES, 2 * LANES), 2 * LANES)
            rowexp[:, at] = jnp.dot(rsplit[...], emat[:, at], preferred_element_type=F32)
            return carry

        lax.fori_loop(0, half // (2 * LANES), expand, 0)

    def station_terms(phase):
        def tile_step(step, carry):
            g = step // (nb // 16)
            part = lax.rem(step, nb // 16)
            lanes = pl.ds(pl.multiple_of(g * LANES, LANES), LANES)
            lanes_low = pl.ds(pl.multiple_of(half + g * LANES, LANES), LANES)
            blocks = pl.ds(pl.multiple_of(part * 16, 16), 16)

            def at(index):
                return pl.ds(pl.multiple_of(index * nb + part * 16, 16), 16)

            model_r = jnp.zeros((16, LANES), F32)
            model_i = jnp.zeros((16, LANES), F32)
            cross = []
            for d in range(ndir):
                for k in range(kl):
                    re, im = d * 2 * kl + k, d * 2 * kl + kl + k
                    coh_r = cohv[d, 0, k, blocks, lanes].astype(F32)
                    coh_i = cohv[d, 1, k, blocks, lanes].astype(F32)
                    col_r, col_i = colg[re, blocks, :], colg[im, blocks, :]
                    cr = coh_r * col_r + coh_i * col_i
                    ci = coh_i * col_r - coh_r * col_i
                    row_r, row_i = rowexp[at(re), lanes], rowexp[at(im), lanes]
                    model_r = model_r + (row_r * cr - row_i * ci)
                    model_i = model_i + (row_r * ci + row_i * cr)
                    cross.append((cr, ci))
            slot = md * half + g * LANES + iota((16, LANES), 1)
            same = rowtile[blocks, :] == coltile[blocks, :]
            diagonal = same & (slot // TILE == jnp.bitwise_and(slot, TILE - 1))
            inside = slot.astype(F32) < limit[blocks, :]
            valid = jnp.where(inside & jnp.logical_not(diagonal), 1.0, 0.0)
            res_r = valid * (visv[0, blocks, lanes].astype(F32) - model_r)
            res_i = valid * (visv[1, blocks, lanes].astype(F32) - model_i)
            for index, (cr, ci) in enumerate(cross):
                terms = (
                    res_r * cr + res_i * ci,
                    res_i * cr - res_r * ci,
                    valid * (cr * cr + ci * ci),
                )
                for q, term in enumerate(terms):
                    high, low = two_pieces(term)
                    tbuf[at(q * kall + index), lanes] = high
                    tbuf[at(q * kall + index), lanes_low] = low
            return carry

        lax.fori_loop(0, (half // LANES) * (nb // 16), tile_step, 0)

        def reduce_step(step, carry):
            q = step // ndir
            d = lax.rem(step, ndir)
            at = pl.ds(pl.multiple_of(step * kl * nb, kl * nb), kl * nb)
            by_block = jnp.dot(tbuf[at, :], rmat[...], preferred_element_type=F32)
            high, low = two_pieces(by_block)
            placed = jnp.dot(
                jnp.concatenate([high, low], axis=1), imat[...], preferred_element_type=F32
            )
            kept = placed.reshape(kl, nb, stations) * amask[...][None]
            summed = jnp.sum(kept, axis=1)
            for b in range(nbl):
                psend[phase, b, d, q, 0:kl, :] = summed[:, b * n : (b + 1) * n]
            return carry

        lax.fori_loop(0, 3 * ndir, reduce_step, 0)

    mine_basis = basis_at(chan, nchan, coefficients)

    def center_of(phase):
        total = jnp.zeros((2, PAD, n), F32)
        for offset in range(nchan):
            source = chan_peer(offset)
            theirs = basis_at(source, nchan, coefficients)
            scale = sum(a * b for a, b in zip(mine_basis, theirs))
            total = total + scale * cbuf[phase, source]
        return total

    for iteration in range(ITERS):
        arrive(gains)
        spread_gains(iteration)
        if iteration == 0:
            for copy in local:
                copy.wait()
            arrive(halves)
        station_terms(iteration)
        moved = term_copies(iteration)
        start(moved)
        everything.append(moved)
        arrive(sums)
        center = center_of(iteration)
        if iteration > 0:
            dual_now = dual_now + gain_now - center
        target = center - dual_now
        arrive(moved)
        terms = psend[iteration, mb, md]
        for offset in range(1, nown):
            sb, sd = group_peer(offset)
            terms = terms + prec[iteration, sb, sd]
        weight = terms[2]
        denominator = weight + stiffness
        gain_now = jnp.stack(
            [
                (terms[c] + gain_now[c] * weight + stiffness * target[c]) / denominator
                for c in range(2)
            ]
        )
        cbuf[iteration + 1, chan] = gain_now + dual_now
        if iteration + 1 < ITERS:
            gbuf[iteration + 1, mb, md] = gain_now
            gains = gain_copies(iteration + 1)
            start(gains)
            everything.append(gains)
        sums = chan_copies(iteration + 1)
        start(sums)
        everything.append(sums)
    gout_ref[:, 0, :, :] = gain_now[:, 0:kl, :]
    arrive(sums)
    center = center_of(ITERS)
    dual_now = dual_now + gain_now - center
    dout_ref[:, 0, :, :] = dual_now[:, 0:kl, :]
    for copies in everything:
        finish(copies)


def on_device(
    nchan, nbl, ndir,
    visibility, coherency, gain_start, dual_start, penalty, tile_pairs, valid_counts, station_order,
):
    kl = gain_start.shape[2]
    n = gain_start.shape[3]
    nb = tile_pairs.shape[0]
    stations = nbl * n
    half = TILE * TILE // ndir
    kall = ndir * kl
    ntile = stations // TILE
    nown = nbl * ndir
    vmem = pl.BlockSpec(memory_space=pltpu.VMEM)
    smem = pl.BlockSpec(memory_space=pltpu.SMEM)
    hbm = pl.BlockSpec(memory_space=pl.ANY)
    dma = pltpu.SemaphoreType.DMA
    out = jax.ShapeDtypeStruct(gain_start.shape, F32)
    return pl.pallas_call(
        functools.partial(kernel, nchan, nbl, ndir, poly_coefficients(nchan)),
        out_shape=(out, out),
        in_specs=[hbm, hbm, vmem, vmem, smem, vmem, vmem, vmem],
        out_specs=(vmem, vmem),
        scratch_shapes=[
            pltpu.VMEM((ndir, 2, kl, nb, half), BF16),
            pltpu.VMEM((2, nb, half), BF16),
            pltpu.VMEM((ITERS, nbl, ndir, 2, PAD, n), F32),
            pltpu.VMEM((ITERS + 1, nchan, 2, PAD, n), F32),
            pltpu.VMEM((ITERS, nbl, ndir, 3, PAD, n), F32),
            pltpu.VMEM((ITERS, nbl, ndir, 3, PAD, n), F32),
            pltpu.VMEM((2, PAD, n), F32),
            pltpu.VMEM((ndir * 2 * PAD, ntile * LANES), F32),
            pltpu.VMEM((ntile * LANES, stations), BF16),
            pltpu.VMEM((2 * LANES, half), BF16),
            pltpu.VMEM((2 * half, LANES), BF16),
            pltpu.VMEM((2 * LANES, stations), BF16),
            pltpu.VMEM((nb, stations), F32),
            pltpu.VMEM((2 * kall, nb, LANES), F32),
            pltpu.VMEM((2 * kall * nb, 2 * LANES), BF16),
            pltpu.VMEM((2 * kall * nb, half), F32),
            pltpu.VMEM((3 * kall * nb, 2 * half), BF16),
            pltpu.VMEM((nb, LANES), jnp.int32),
            pltpu.VMEM((nb, LANES), jnp.int32),
            pltpu.VMEM((nb, LANES), F32),
            dma((2,)),
            dma((ndir,)),
            dma((ndir,)),
            dma((ITERS, nown)),
            dma((ITERS, nown)),
            dma((ITERS + 1, nchan)),
            dma((ITERS + 1, nchan)),
            dma((ITERS, nown)),
            dma((ITERS, nown)),
        ],
        compiler_params=pltpu.CompilerParams(
            collective_id=0, has_side_effects=True, vmem_limit_bytes=48 * 1024 * 1024
        ),
    )(
        coherency,
        visibility,
        gain_start,
        dual_start,
        penalty,
        tile_pairs,
        valid_counts.reshape(1, nb),
        station_order.reshape(1, stations),
    )


def solution(mesh):
    sizes = mesh.shape
    return jax.shard_map(
        functools.partial(on_device, sizes["chan"], sizes["bl"], sizes["dir"]),
        mesh=mesh,
        in_specs=(
            P(None, ("grp", "chan"), "bl", None),
            P(None, ("grp", "chan"), "dir", "bl", None),
            P(None, ("grp", "chan"), "dir", "bl"),
            P(None, ("grp", "chan"), "dir", "bl"),
            P(("grp", "dir")),
            P(("grp", "bl"), None),
            P(("grp", "bl")),
            P("grp"),
        ),
        out_specs=(P(None, ("grp", "chan"), "dir", "bl"), P(None, ("grp", "chan"), "dir", "bl")),
        check_vma=False,
    )
```

profile of v0, /device:TPU:0, one launch (start us, length us, event | category | flops | bytes accessed | tf_op | source)
XLA Modules:
  0.0 54.4 jit_solution(14153000603768433512)
XLA Ops:
  0.6 0.7 %copy.10.gain_ref = f32[2,1,5,256]{3,2,1,0:T(8,128)S(1)} copy(f32[2,1,5,256]{3,1,2,0:T(1,128)} %param.10) | data formatting | bytes 20480 | tf_op args[2]
  1.3 0.7 %copy.11.dual_ref = f32[2,1,5,256]{3,2,1,0:T(8,128)S(1)} copy(f32[2,1,5,256]{3,1,2,0:T(1,128)} %param.11) | data formatting | bytes 20480 | tf_op args[3]
  2.0 0.8 %copy.12.pairs_ref = s32[32,2]{1,0:T(8,128)S(1)} copy(s32[32,2]{0,1:T(2,128)} %param.13) | data formatting | bytes 512 | tf_op args[5]
  2.8 0.0 copy-start
  2.8 1.7 %copy-done = bf16[2,1,5,32,4096]{4,3,2,1,0:T(8,128)(2,1)S(1)} copy-done((bf16[2,1,5,32,4096]{4,3,2,1,0:T(8,128)(2,1)S(1)}, bf16[2,1,5,32,4096]{4,3,2,1,0:T(8,128)(2,1)}, u32[]{:S(2)}) %copy-start) | copy-done | bytes 2621464
  4.5 0.0 copy-start.1
  4.5 1.0 %copy-done.1 = bf16[2,1,32,4096]{3,2,1,0:T(8,128)(2,1)S(1)} copy-done((bf16[2,1,32,4096]{3,2,1,0:T(8,128)(2,1)S(1)}, bf16[2,1,32,4096]{3,2,1,0:T(8,128)(2,1)}, u32[]{:S(2)}) %copy-start.1) | copy-done | bytes 524312
  5.6 0.0 copy-start.2
  5.6 0.7 %copy-done.2 = s32[512]{0:T(512)S(1)} copy-done((s32[512]{0:T(512)S(1)}, s32[512]{0:T(512)}, u32[]{:S(2)}) %copy-start.2) | copy-done | bytes 2072
  6.3 0.0 copy-start.3
  6.3 0.7 %copy-done.3 = f32[5]{0:T(128)S(1)} copy-done((f32[5]{0:T(128)S(1)}, f32[5]{0:T(128)}, u32[]{:S(2)}) %copy-start.3) | copy-done | bytes 44
  6.9 0.0 copy-start.4
  6.9 0.7 %copy-done.4 = s32[32]{0:T(128)S(1)} copy-done((s32[32]{0:T(128)S(1)}, s32[32]{0:T(128)}, u32[]{:S(2)}) %copy-start.4) | copy-done | bytes 152
  7.6 45.5 %shard_map.95 = (f32[2,1,5,256]{3,2,1,0:T(8,128)S(1)}, f32[2,1,5,256]{3,2,1,0:T(8,128)S(1)}) custom-call(bf16[2,1,5,32,4096]{4,3,2,1,0:T(8,128)(2,1)S(1)} %copy-done, bf16[2,1,32,4096]{3,2,1,0:T(8,128)(2,1)S(1)} %copy-done.1, f32[2,1,5,256]{3,2,1,0:T(8,128)S(1)} %copy.10.gain_ref, f32[2,1,5,256]{3,2,1,0:T(8,128)S(1)} %copy.11.dual_ref, f32[5]{0:T(128)S(1)} %copy-done.3, ...), custom_call_target="tpu_custom_call" | custom-call | tf_op jit(solution)/shard_map/pallas_call | solution.py:419
  53.1 0.6 %copy.13 = f32[2,1,5,256]{3,1,2,0:T(1,128)} copy(f32[2,1,5,256]{3,2,1,0:T(8,128)S(1)} %get-tuple-element.2) | data formatting | bytes 20480 | tf_op jit(solution)/shard_map/pallas_call | solution.py:419
  53.7 0.6 %copy.14 = f32[2,1,5,256]{3,1,2,0:T(1,128)} copy(f32[2,1,5,256]{3,2,1,0:T(8,128)S(1)} %get-tuple-element.3) | data formatting | bytes 20480 | tf_op jit(solution)/shard_map/pallas_call | solution.py:419
Async XLA Ops:
  2.8 1.7 %copy-start = (bf16[2,1,5,32,4096]{4,3,2,1,0:T(8,128)(2,1)S(1)}, bf16[2,1,5,32,4096]{4,3,2,1,0:T(8,128)(2,1)}, u32[]{:S(2)}) copy-start(bf16[2,1,5,32,4096]{4,3,2,1,0:T(8,128)(2,1)} %coh_hbm.1) | copy-start | bytes 7864324
  4.5 1.0 %copy-start.1 = (bf16[2,1,32,4096]{3,2,1,0:T(8,128)(2,1)S(1)}, bf16[2,1,32,4096]{3,2,1,0:T(8,128)(2,1)}, u32[]{:S(2)}) copy-start(bf16[2,1,32,4096]{3,2,1,0:T(8,128)(2,1)} %vis_hbm.1) | copy-start | bytes 1572868
  5.6 0.7 %copy-start.2 = (s32[512]{0:T(512)S(1)}, s32[512]{0:T(512)}, u32[]{:S(2)}) copy-start(s32[512]{0:T(512)} %param.15) | copy-start | bytes 6148
  6.3 0.7 %copy-start.3 = (f32[5]{0:T(128)S(1)}, f32[5]{0:T(128)}, u32[]{:S(2)}) copy-start(f32[5]{0:T(128)} %pen_ref.1) | copy-start | bytes 64
  6.9 0.7 %copy-start.4 = (s32[32]{0:T(128)S(1)}, s32[32]{0:T(128)}, u32[]{:S(2)}) copy-start(s32[32]{0:T(128)} %param.14) | copy-start | bytes 388
where the time goes:
time: 54.7 us; the launch traced here: 54.4 us
  Pallas kernels  45.5 us (83%)
  local copies, waits for them, and re-layouts  8.16 us (15%)
  between operations  0.64 us (1%)
    pallas_call x1, Pallas kernels, on_device(): pl.pallas_call(functools.partial(kernel, nchan, nbl, ndir, poly_coefficie...  45.5 us
    unnamed x13, local copies, waits for them, and re-layouts  6.94 us
    pallas_call x2, local copies, waits for them, and re-layouts, on_device(): pl.pallas_call(functools.partial(kernel, nchan, nbl, ndir, poly_coefficie...  1.22 us

commit v1 on v0

--- a/solution.py
+++ b/solution.py
@@ -13,6 +13,8 @@
 ITERS = 2
 LANES = 128
 PAD = 8
+FOLD = 4
+GROUP = FOLD * LANES
 MESH = pl.DeviceIdType.MESH
 F32 = jnp.float32
 BF16 = jnp.bfloat16
@@ -56,10 +58,11 @@
 
 def kernel(
     nchan, nbl, ndir, coefficients,
-    coh_hbm, vis_hbm, gain_ref, dual_ref, pen_ref, pairs_ref, cnt_ref, ord_ref,
+    coh_hbm, vis_hbm, gain_hbm, dual_hbm, pen_ref, pairs_hbm, cnt_hbm, ord_hbm,
     gout_ref, dout_ref,
-    cohv, visv, gbuf, cbuf, psend, prec, dualp, natscr, dmat, emat, rmat, imat, amask,
-    colg, rsplit, rowexp, tbuf, rowtile, coltile, limit,
+    cohv, visv, cohp, visp, gain_ref, dual_ref, pairs_ref, cnt_ref, ord_ref,
+    gbuf, cbuf, psend, prec, dualp, natscr, dmat, perm, rowmat, colmat, rmat, imat, amask,
+    rsplit, csplit, rowexp, colexp, tbuf, rowtile, coltile, limit,
     lsem, hsend, hrecv, gsend, grecv, csend, crecv, psems, precv,
 ):
     chan = lax.axis_index("chan")
@@ -67,15 +70,18 @@
     md = lax.axis_index("dir")
     mine = mb * ndir + md
     nown = nbl * ndir
-    kl = gain_ref.shape[2]
-    n = gain_ref.shape[3]
+    kl = gain_hbm.shape[1]
+    n = gain_hbm.shape[3]
     stations = nbl * n
-    nb = pairs_ref.shape[0]
+    nb = pairs_hbm.shape[1]
     slots = TILE * TILE
     half = slots // ndir
     rows_half = half // TILE
     ntile = stations // TILE
     kall = ndir * kl
+    ngroup = half // GROUP
+    rows_group = LANES * FOLD // TILE
+    per_row = LANES // rows_group
 
     def group_peer(offset):
         peer = lax.rem(mine + offset, nown)
@@ -87,11 +93,23 @@
     def own_half():
         return pl.ds(pl.multiple_of(md * half, half), half)
 
+    small = [
+        pltpu.make_async_copy(source, target, lsem.at[2 + index])
+        for index, (source, target) in enumerate(
+            [
+                (gain_hbm, gain_ref),
+                (dual_hbm, dual_ref),
+                (pairs_hbm, pairs_ref),
+                (cnt_hbm, cnt_ref),
+                (ord_hbm, ord_ref),
+            ]
+        )
+    ]
     local = [
         pltpu.make_async_copy(coh_hbm.at[:, 0, :, :, own_half()], cohv.at[md], lsem.at[0]),
         pltpu.make_async_copy(vis_hbm.at[:, 0, :, own_half()], visv, lsem.at[1]),
     ]
-    for copy in local:
+    for copy in small + local:
         copy.start()
 
     barrier = pltpu.get_barrier_semaphore()
@@ -106,9 +124,12 @@
     gbuf[0, mb, md] = jnp.zeros((2, PAD, n), F32)
     dualp[...] = jnp.zeros((2, PAD, n), F32)
     psend[...] = jnp.zeros(psend.shape, F32)
+    for copy in small:
+        copy.wait()
     for c in range(2):
-        gbuf[0, mb, md, c, 0:kl, :] = gain_ref[c, 0]
-        dualp[c, 0:kl, :] = dual_ref[c, 0]
+        for k in range(kl):
+            gbuf[0, mb, md, c, k : k + 1, :] = gain_ref[c, k]
+            dualp[c, k : k + 1, :] = dual_ref[c, k]
     gain_now = gbuf[0, mb, md]
     dual_now = dualp[...]
     cbuf[0, chan] = gain_now + dual_now
@@ -208,23 +229,40 @@
     order = ord_ref[...]
     wide = iota((ntile * LANES, stations), 0)
     dmat[...] = onehot(jnp.bitwise_and(wide, TILE - 1) + (wide // LANES) * TILE == order)
-    shape = (2 * LANES, half)
-    emat[...] = onehot(
-        jnp.bitwise_and(iota(shape, 0), LANES - 1) == md * rows_half + iota(shape, 1) // TILE
+    shape = (GROUP, GROUP)
+    to_lane = jnp.bitwise_and(iota(shape, 1), LANES - 1)
+    from_lane = (to_lane // per_row) * TILE + (iota(shape, 1) // LANES) * per_row
+    perm[...] = onehot(iota(shape, 0) == from_lane + jnp.bitwise_and(to_lane, per_row - 1))
+    shape = (2 * LANES, ngroup * LANES)
+    to_lane = iota(shape, 1)
+    from_row = jnp.where(
+        iota(shape, 0) < 3 * TILE, jnp.bitwise_and(iota(shape, 0), TILE - 1), slots
     )
-    shape = (2 * half, LANES)
-    rmat[...] = onehot(jnp.bitwise_and(iota(shape, 0), half - 1) // TILE == iota(shape, 1))
+    rowmat[...] = onehot(from_row == md * rows_half + to_lane // per_row)
+    shape = (2 * LANES, GROUP)
+    to_lane = iota(shape, 1)
+    from_row = jnp.where(
+        iota(shape, 0) < 3 * TILE, jnp.bitwise_and(iota(shape, 0), TILE - 1), slots
+    )
+    colmat[...] = onehot(
+        from_row == (to_lane // LANES) * per_row + jnp.bitwise_and(to_lane, per_row - 1)
+    )
+    shape = (ngroup * LANES, LANES)
+    rmat[0 : ngroup * LANES, :] = onehot(iota(shape, 0) // per_row == iota(shape, 1))
+    rmat[ngroup * LANES :, :] = onehot(iota(shape, 0) // per_row == iota(shape, 1))
     row_in = jnp.bitwise_and(iota((2 * LANES, stations), 0), LANES - 1)
     imat[...] = onehot(
         (row_in < rows_half) & (row_in + md * rows_half == jnp.bitwise_and(order, TILE - 1))
     )
-    amask[...] = jnp.where(order // TILE == pairs_ref[:, 0:1], 1.0, 0.0)
-    rowtile[...] = jnp.broadcast_to(pairs_ref[:, 0:1], (nb, LANES))
-    coltile[...] = jnp.broadcast_to(pairs_ref[:, 1:2], (nb, LANES))
-    square = jnp.where(
-        iota((nb, nb), 0) == iota((nb, nb), 1), cnt_ref[...].astype(F32), 0.0
-    )
-    limit[...] = jnp.broadcast_to(jnp.sum(square, axis=1, keepdims=True), (nb, LANES))
+    def column(row):
+        square = jnp.where(iota((nb, nb), 0) == iota((nb, nb), 1), row.astype(F32), 0.0)
+        return jnp.sum(square, axis=1, keepdims=True)
+
+    row_column = column(pairs_ref[0:1, :])
+    rowtile[...] = jnp.broadcast_to(row_column, (nb, LANES))
+    coltile[...] = jnp.broadcast_to(column(pairs_ref[1:2, :]), (nb, LANES))
+    limit[...] = jnp.broadcast_to(column(cnt_ref[...]), (nb, LANES))
+    amask[...] = jnp.where((order // TILE).astype(F32) == row_column, 1.0, 0.0)
 
     row_k = iota((PAD, n), 0)
     stiffness = jnp.ones((PAD, n), F32)
@@ -259,87 +297,111 @@
             by_col = jnp.zeros((nb, LANES), F32)
             for t in range(ntile):
                 tile = values[:, t * LANES : (t + 1) * LANES]
-                by_row = jnp.where(rowtile[...] == t, tile, by_row)
-                by_col = jnp.where(coltile[...] == t, tile, by_col)
-            colg[index] = by_col
-            high, low = two_pieces(by_row)
+                by_row = jnp.where(rowtile[...] == float(t), tile, by_row)
+                by_col = jnp.where(coltile[...] == float(t), tile, by_col)
             at = pl.ds(pl.multiple_of(index * nb, nb), nb)
-            rsplit[at, 0:LANES] = high
-            rsplit[at, LANES : 2 * LANES] = low
+            low_lanes = iota((nb, LANES), 1) < TILE
+            for gains_of, split in ((by_row, rsplit), (by_col, csplit)):
+                first, rest = two_pieces(gains_of)
+                rest = gains_of - first.astype(F32)
+                second, third = two_pieces(rest)
+                split[at, 0:LANES] = jnp.where(
+                    low_lanes, first.astype(F32), second.astype(F32)
+                ).astype(BF16)
+                split[at, LANES : 2 * LANES] = third
             return carry
 
         lax.fori_loop(0, 2 * kall, one, 0)
-
-        def expand(step, carry):
-            at = pl.ds(pl.multiple_of(step * 2 * LANES, 2 * LANES), 2 * LANES)
-            rowexp[:, at] = jnp.dot(rsplit[...], emat[:, at], preferred_element_type=F32)
+        rowexp[...] = jnp.dot(rsplit[...], rowmat[...], preferred_element_type=F32)
+        colexp[...] = jnp.dot(csplit[...], colmat[...], preferred_element_type=F32)
+
+    def permute_half(d):
+        def step(g, carry):
+            lanes = pl.ds(pl.multiple_of(g * GROUP, GROUP), GROUP)
+            source = cohv[d, :, :, :, lanes].reshape(2 * kl * nb, GROUP)
+            moved = jnp.dot(source, perm[...], preferred_element_type=F32)
+            cohp[d, :, :, :, lanes] = moved.reshape(2, kl, nb, GROUP)
             return carry
 
-        lax.fori_loop(0, half // (2 * LANES), expand, 0)
+        lax.fori_loop(0, ngroup, step, 0)
+
+    def permute_vis():
+        def step(g, carry):
+            lanes = pl.ds(pl.multiple_of(g * GROUP, GROUP), GROUP)
+            source = visv[:, :, lanes].reshape(2 * nb, GROUP)
+            moved = jnp.dot(source, perm[...], preferred_element_type=F32)
+            visp[:, :, lanes] = moved.reshape(2, nb, GROUP)
+            return carry
+
+        lax.fori_loop(0, ngroup, step, 0)
 
     def station_terms(phase):
         def tile_step(step, carry):
-            g = step // (nb // 16)
-            part = lax.rem(step, nb // 16)
+            g = step // (nb // PAD)
+            part = lax.rem(step, nb // PAD)
             lanes = pl.ds(pl.multiple_of(g * LANES, LANES), LANES)
-            lanes_low = pl.ds(pl.multiple_of(half + g * LANES, LANES), LANES)
-            blocks = pl.ds(pl.multiple_of(part * 16, 16), 16)
+            blocks = pl.ds(pl.multiple_of(part * PAD, PAD), PAD)
 
             def at(index):
-                return pl.ds(pl.multiple_of(index * nb + part * 16, 16), 16)
-
-            model_r = jnp.zeros((16, LANES), F32)
-            model_i = jnp.zeros((16, LANES), F32)
-            cross = []
-            for d in range(ndir):
-                for k in range(kl):
-                    re, im = d * 2 * kl + k, d * 2 * kl + kl + k
-                    coh_r = cohv[d, 0, k, blocks, lanes].astype(F32)
-                    coh_i = cohv[d, 1, k, blocks, lanes].astype(F32)
-                    col_r, col_i = colg[re, blocks, :], colg[im, blocks, :]
-                    cr = coh_r * col_r + coh_i * col_i
-                    ci = coh_i * col_r - coh_r * col_i
-                    row_r, row_i = rowexp[at(re), lanes], rowexp[at(im), lanes]
-                    model_r = model_r + (row_r * cr - row_i * ci)
-                    model_i = model_i + (row_r * ci + row_i * cr)
-                    cross.append((cr, ci))
-            slot = md * half + g * LANES + iota((16, LANES), 1)
+                return pl.ds(pl.multiple_of(index * nb + part * PAD, PAD), PAD)
+
+            lane = iota((PAD, LANES), 1)
+            row = md * rows_half + g * rows_group + lane // per_row
             same = rowtile[blocks, :] == coltile[blocks, :]
-            diagonal = same & (slot // TILE == jnp.bitwise_and(slot, TILE - 1))
-            inside = slot.astype(F32) < limit[blocks, :]
-            valid = jnp.where(inside & jnp.logical_not(diagonal), 1.0, 0.0)
-            res_r = valid * (visv[0, blocks, lanes].astype(F32) - model_r)
-            res_i = valid * (visv[1, blocks, lanes].astype(F32) - model_i)
-            for index, (cr, ci) in enumerate(cross):
-                terms = (
-                    res_r * cr + res_i * ci,
-                    res_i * cr - res_r * ci,
-                    valid * (cr * cr + ci * ci),
-                )
-                for q, term in enumerate(terms):
-                    high, low = two_pieces(term)
-                    tbuf[at(q * kall + index), lanes] = high
-                    tbuf[at(q * kall + index), lanes_low] = low
+            totals = [jnp.zeros((PAD, LANES), F32)] * (3 * kall)
+            for v in range(FOLD):
+                here = pl.ds(pl.multiple_of(g * GROUP + v * LANES, LANES), LANES)
+                cols = slice(v * LANES, (v + 1) * LANES)
+                model_r = jnp.zeros((PAD, LANES), F32)
+                model_i = jnp.zeros((PAD, LANES), F32)
+                cross = []
+                for d in range(ndir):
+                    for k in range(kl):
+                        re, im = d * 2 * kl + k, d * 2 * kl + kl + k
+                        coh_r = cohp[d, 0, k, blocks, here]
+                        coh_i = cohp[d, 1, k, blocks, here]
+                        col_r, col_i = colexp[at(re), cols], colexp[at(im), cols]
+                        cr = coh_r * col_r + coh_i * col_i
+                        ci = coh_i * col_r - coh_r * col_i
+                        row_r, row_i = rowexp[at(re), lanes], rowexp[at(im), lanes]
+                        model_r = model_r + (row_r * cr - row_i * ci)
+                        model_i = model_i + (row_r * ci + row_i * cr)
+                        cross.append((cr, ci))
+                col = v * per_row + jnp.bitwise_and(lane, per_row - 1)
+                inside = (row * TILE + col).astype(F32) < limit[blocks, :]
+                valid = jnp.where(inside & jnp.logical_not(same & (row == col)), 1.0, 0.0)
+                res_r = valid * (visp[0, blocks, here] - model_r)
+                res_i = valid * (visp[1, blocks, here] - model_i)
+                for index, (cr, ci) in enumerate(cross):
+                    terms = (
+                        res_r * cr + res_i * ci,
+                        res_i * cr - res_r * ci,
+                        valid * (cr * cr + ci * ci),
+                    )
+                    for q, term in enumerate(terms):
+                        totals[q * kall + index] = totals[q * kall + index] + term
+            for index, total in enumerate(totals):
+                tbuf[at(index), lanes] = total
             return carry
 
-        lax.fori_loop(0, (half // LANES) * (nb // 16), tile_step, 0)
-
-        def reduce_step(step, carry):
-            q = step // ndir
-            d = lax.rem(step, ndir)
-            at = pl.ds(pl.multiple_of(step * kl * nb, kl * nb), kl * nb)
-            by_block = jnp.dot(tbuf[at, :], rmat[...], preferred_element_type=F32)
+        lax.fori_loop(0, ngroup * (nb // PAD), tile_step, 0)
+
+        for q in range(3):
+            high, low = two_pieces(tbuf[q * kall * nb : (q + 1) * kall * nb, :])
+            by_block = jnp.dot(
+                jnp.concatenate([high, low], axis=1), rmat[...], preferred_element_type=F32
+            )
             high, low = two_pieces(by_block)
             placed = jnp.dot(
                 jnp.concatenate([high, low], axis=1), imat[...], preferred_element_type=F32
             )
-            kept = placed.reshape(kl, nb, stations) * amask[...][None]
+            kept = placed.reshape(kall, nb, stations) * amask[...][None]
             summed = jnp.sum(kept, axis=1)
-            for b in range(nbl):
-                psend[phase, b, d, q, 0:kl, :] = summed[:, b * n : (b + 1) * n]
-            return carry
-
-        lax.fori_loop(0, 3 * ndir, reduce_step, 0)
+            for d in range(ndir):
+                for b in range(nbl):
+                    psend[phase, b, d, q, 0:kl, :] = summed[
+                        d * kl : (d + 1) * kl, b * n : (b + 1) * n
+                    ]
 
     mine_basis = basis_at(chan, nchan, coefficients)
 
@@ -353,12 +415,17 @@
         return total
 
     for iteration in range(ITERS):
+        if iteration == 0:
+            for copy in local:
+                copy.wait()
+            permute_half(md)
+            permute_vis()
         arrive(gains)
         spread_gains(iteration)
         if iteration == 0:
-            for copy in local:
-                copy.wait()
             arrive(halves)
+            for offset in range(1, ndir):
+                permute_half(lax.rem(md + offset, ndir))
         station_terms(iteration)
         moved = term_copies(iteration)
         start(moved)
@@ -390,11 +457,15 @@
         sums = chan_copies(iteration + 1)
         start(sums)
         everything.append(sums)
-    gout_ref[:, 0, :, :] = gain_now[:, 0:kl, :]
+    for c in range(2):
+        for k in range(kl):
+            gout_ref[c, k] = gain_now[c, k : k + 1, :]
     arrive(sums)
     center = center_of(ITERS)
     dual_now = dual_now + gain_now - center
-    dout_ref[:, 0, :, :] = dual_now[:, 0:kl, :]
+    for c in range(2):
+        for k in range(kl):
+            dout_ref[c, k] = dual_now[c, k : k + 1, :]
     for copies in everything:
         finish(copies)
 
@@ -415,15 +486,23 @@
     smem = pl.BlockSpec(memory_space=pltpu.SMEM)
     hbm = pl.BlockSpec(memory_space=pl.ANY)
     dma = pltpu.SemaphoreType.DMA
-    out = jax.ShapeDtypeStruct(gain_start.shape, F32)
-    return pl.pallas_call(
+    out = jax.ShapeDtypeStruct((2, kl, 1, n), F32)
+    ngroup = half // GROUP
+    gain, dual = pl.pallas_call(
         functools.partial(kernel, nchan, nbl, ndir, poly_coefficients(nchan)),
         out_shape=(out, out),
-        in_specs=[hbm, hbm, vmem, vmem, smem, vmem, vmem, vmem],
+        in_specs=[hbm, hbm, hbm, hbm, smem, hbm, hbm, hbm],
         out_specs=(vmem, vmem),
         scratch_shapes=[
             pltpu.VMEM((ndir, 2, kl, nb, half), BF16),
             pltpu.VMEM((2, nb, half), BF16),
+            pltpu.VMEM((ndir, 2, kl, nb, half), F32),
+            pltpu.VMEM((2, nb, half), F32),
+            pltpu.VMEM((2, kl, 1, n), F32),
+            pltpu.VMEM((2, kl, 1, n), F32),
+            pltpu.VMEM((2, nb), jnp.int32),
+            pltpu.VMEM((1, nb), jnp.int32),
+            pltpu.VMEM((1, stations), jnp.int32),
             pltpu.VMEM((ITERS, nbl, ndir, 2, PAD, n), F32),
             pltpu.VMEM((ITERS + 1, nchan, 2, PAD, n), F32),
             pltpu.VMEM((ITERS, nbl, ndir, 3, PAD, n), F32),
@@ -431,18 +510,21 @@
             pltpu.VMEM((2, PAD, n), F32),
             pltpu.VMEM((ndir * 2 * PAD, ntile * LANES), F32),
             pltpu.VMEM((ntile * LANES, stations), BF16),
-            pltpu.VMEM((2 * LANES, half), BF16),
-            pltpu.VMEM((2 * half, LANES), BF16),
+            pltpu.VMEM((GROUP, GROUP), BF16),
+            pltpu.VMEM((2 * LANES, ngroup * LANES), BF16),
+            pltpu.VMEM((2 * LANES, GROUP), BF16),
+            pltpu.VMEM((2 * ngroup * LANES, LANES), BF16),
             pltpu.VMEM((2 * LANES, stations), BF16),
             pltpu.VMEM((nb, stations), F32),
-            pltpu.VMEM((2 * kall, nb, LANES), F32),
             pltpu.VMEM((2 * kall * nb, 2 * LANES), BF16),
-            pltpu.VMEM((2 * kall * nb, half), F32),
-            pltpu.VMEM((3 * kall * nb, 2 * half), BF16),
-            pltpu.VMEM((nb, LANES), jnp.int32),
-            pltpu.VMEM((nb, LANES), jnp.int32),
+            pltpu.VMEM((2 * kall * nb, 2 * LANES), BF16),
+            pltpu.VMEM((2 * kall * nb, ngroup * LANES), F32),
+            pltpu.VMEM((2 * kall * nb, GROUP), F32),
+            pltpu.VMEM((3 * kall * nb, ngroup * LANES), F32),
             pltpu.VMEM((nb, LANES), F32),
-            dma((2,)),
+            pltpu.VMEM((nb, LANES), F32),
+            pltpu.VMEM((nb, LANES), F32),
+            dma((7,)),
             dma((ndir,)),
             dma((ndir,)),
             dma((ITERS, nown)),
@@ -453,18 +535,19 @@
             dma((ITERS, nown)),
         ],
         compiler_params=pltpu.CompilerParams(
-            collective_id=0, has_side_effects=True, vmem_limit_bytes=48 * 1024 * 1024
+            collective_id=0, has_side_effects=True, vmem_limit_bytes=60 * 1024 * 1024
         ),
     )(
         coherency,
         visibility,
-        gain_start,
-        dual_start,
+        jnp.transpose(gain_start, (0, 2, 1, 3)),
+        jnp.transpose(dual_start, (0, 2, 1, 3)),
         penalty,
-        tile_pairs,
+        tile_pairs.T,
         valid_counts.reshape(1, nb),
         station_order.reshape(1, stations),
     )
+    return jnp.transpose(gain, (0, 2, 1, 3)), jnp.transpose(dual, (0, 2, 1, 3))
 
 
 def solution(mesh):

time: 54.7 us -> 41.2 us (0.75)
  Pallas kernels: 45.5 us -> 37.6 us
  local copies, waits for them, and re-layouts: 8.16 us -> 2.6 us
    pallas_call x1, Pallas kernels: 45.5 us -> 37.6 us  [on_device(): pl.pallas_call(functools.partial(kernel, nchan, nbl, ndir, poly_coefficie...]
    unnamed x13 -> x2, local copies, waits for them, and re-layouts: 6.94 us -> 2.6 us
    pallas_call x2 -> x0, local copies, waits for them, and re-layouts: 1.22 us -> none  [on_device(): pl.pallas_call(functools.partial(kernel, nchan, nbl, ndir, poly_coefficie...]
where the time goes in v1:
time: 41.2 us; the launch traced here: 40.9 us
  Pallas kernels  37.6 us (91%)
  local copies, waits for them, and re-layouts  2.6 us (6%)
  between operations  0.64 us (2%)
    pallas_call x1, Pallas kernels, on_device(): pl.pallas_call(functools.partial(kernel, nchan, nbl, ndir, poly_coefficie...  37.6 us
    unnamed x2, local copies, waits for them, and re-layouts  2.6 us

profile of v1, /device:TPU:0, one launch (start us, length us, event | category | flops | bytes accessed | tf_op | source)
XLA Modules:
  0.0 40.9 jit_solution(8675570965989220072)
XLA Ops:
  0.6 37.6 %shard_map.95 = (f32[2,5,1,256]{3,2,1,0:T(1,128)}, f32[2,5,1,256]{3,2,1,0:T(1,128)}) custom-call(bf16[2,1,5,32,4096]{4,3,2,1,0:T(8,128)(2,1)} %coh_hbm.1, bf16[2,1,32,4096]{3,2,1,0:T(8,128)(2,1)} %vis_hbm.1, f32[2,5,1,256]{3,2,1,0:T(1,128)} %bitcast.7, f32[2,5,1,256]{3,2,1,0:T(1,128)} %bitcast.8, f32[5]{0:T(128)} %pen_ref.1, s32[2,32]{1,0:T(2,128)} %bitcast.12, ...), custom_call_target="tpu_custom_call" | custom-call | tf_op jit(solution)/shard_map/pallas_call | solution.py:491
  38.3 1.3 %copy.12 = f32[2,1,5,256]{3,1,2,0:T(1,128)} copy(f32[2,1,5,256]{3,1,2,0:T(1,128)} %bitcast.10) | data formatting | bytes 20480
  39.6 1.3 %copy.13 = f32[2,1,5,256]{3,1,2,0:T(1,128)} copy(f32[2,1,5,256]{3,1,2,0:T(1,128)} %bitcast.9) | data formatting | bytes 20480

commit v2 on v1

--- a/solution.py
+++ b/solution.py
@@ -46,6 +46,10 @@
     return lax.broadcasted_iota(jnp.int32, shape, dim)
 
 
+def shift_of(size):
+    return jnp.int32(size.bit_length() - 1)
+
+
 def onehot(mask):
     return jnp.where(mask, 1.0, 0.0).astype(BF16)
 
@@ -61,8 +65,8 @@
     coh_hbm, vis_hbm, gain_hbm, dual_hbm, pen_ref, pairs_hbm, cnt_hbm, ord_hbm,
     gout_ref, dout_ref,
     cohv, visv, cohp, visp, gain_ref, dual_ref, pairs_ref, cnt_ref, ord_ref,
-    gbuf, cbuf, psend, prec, dualp, natscr, dmat, perm, rowmat, colmat, rmat, imat, amask,
-    rsplit, csplit, rowexp, colexp, tbuf, rowtile, coltile, limit,
+    gbuf, cbuf, psend, prec, dualp, perm, rowmat, colmat, rmat, imat, amask,
+    tilemask, inmat, select, rowexp, colexp, tbuf, rowtile, coltile, limit,
     lsem, hsend, hrecv, gsend, grecv, csend, crecv, psems, precv,
 ):
     chan = lax.axis_index("chan")
@@ -77,7 +81,7 @@
     slots = TILE * TILE
     half = slots // ndir
     rows_half = half // TILE
-    ntile = stations // TILE
+    assert stations // TILE <= PAD
     kall = ndir * kl
     ngroup = half // GROUP
     rows_group = LANES * FOLD // TILE
@@ -227,33 +231,33 @@
     everything += [gains, halves, sums]
 
     order = ord_ref[...]
-    wide = iota((ntile * LANES, stations), 0)
-    dmat[...] = onehot(jnp.bitwise_and(wide, TILE - 1) + (wide // LANES) * TILE == order)
-    shape = (GROUP, GROUP)
-    to_lane = jnp.bitwise_and(iota(shape, 1), LANES - 1)
-    from_lane = (to_lane // per_row) * TILE + (iota(shape, 1) // LANES) * per_row
-    perm[...] = onehot(iota(shape, 0) == from_lane + jnp.bitwise_and(to_lane, per_row - 1))
-    shape = (2 * LANES, ngroup * LANES)
-    to_lane = iota(shape, 1)
-    from_row = jnp.where(
-        iota(shape, 0) < 3 * TILE, jnp.bitwise_and(iota(shape, 0), TILE - 1), slots
+    within = jnp.bitwise_and(order, TILE - 1)
+    tile_of = lax.shift_right_logical(order, shift_of(TILE))
+    tilemask[...] = jnp.where(iota((PAD, stations), 0) == tile_of, 1.0, 0.0)
+    both = iota((LANES, stations), 0)
+    inmat[:, 0:stations] = onehot(both == within)
+    inmat[:, stations : 2 * stations] = onehot(both - TILE == within)
+    to_lane = iota((1, GROUP), 1)
+    lane_row = lax.shift_right_logical(jnp.bitwise_and(to_lane, LANES - 1), shift_of(per_row))
+    lane_col = lax.shift_right_logical(to_lane, shift_of(LANES)) * per_row + jnp.bitwise_and(
+        to_lane, per_row - 1
     )
-    rowmat[...] = onehot(from_row == md * rows_half + to_lane // per_row)
-    shape = (2 * LANES, GROUP)
-    to_lane = iota(shape, 1)
-    from_row = jnp.where(
-        iota(shape, 0) < 3 * TILE, jnp.bitwise_and(iota(shape, 0), TILE - 1), slots
-    )
-    colmat[...] = onehot(
-        from_row == (to_lane // LANES) * per_row + jnp.bitwise_and(to_lane, per_row - 1)
-    )
+    perm[...] = onehot(iota((GROUP, GROUP), 0) == lane_row * TILE + lane_col)
+    piece_row = jnp.bitwise_and(iota((LANES, GROUP), 0), TILE - 1)
+    colmat[...] = onehot(piece_row == lane_col)
+    shape = (LANES, ngroup * LANES)
+    lane_row = lax.shift_right_logical(iota((1, ngroup * LANES), 1), shift_of(per_row))
+    piece_row = jnp.bitwise_and(iota(shape, 0), TILE - 1)
+    rowmat[...] = onehot(piece_row == md * rows_half + lane_row)
     shape = (ngroup * LANES, LANES)
-    rmat[0 : ngroup * LANES, :] = onehot(iota(shape, 0) // per_row == iota(shape, 1))
-    rmat[ngroup * LANES :, :] = onehot(iota(shape, 0) // per_row == iota(shape, 1))
-    row_in = jnp.bitwise_and(iota((2 * LANES, stations), 0), LANES - 1)
-    imat[...] = onehot(
-        (row_in < rows_half) & (row_in + md * rows_half == jnp.bitwise_and(order, TILE - 1))
-    )
+    summing = onehot(lax.shift_right_logical(iota(shape, 0), shift_of(per_row)) == iota(shape, 1))
+    rmat[0 : ngroup * LANES, :] = summing
+    rmat[ngroup * LANES :, :] = summing
+    row_in = iota((LANES, stations), 0)
+    placing = onehot((row_in < rows_half) & (row_in + md * rows_half == within))
+    imat[0:LANES, :] = placing
+    imat[LANES : 2 * LANES, :] = placing
+
     def column(row):
         square = jnp.where(iota((nb, nb), 0) == iota((nb, nb), 1), row.astype(F32), 0.0)
         return jnp.sum(square, axis=1, keepdims=True)
@@ -262,7 +266,10 @@
     rowtile[...] = jnp.broadcast_to(row_column, (nb, LANES))
     coltile[...] = jnp.broadcast_to(column(pairs_ref[1:2, :]), (nb, LANES))
     limit[...] = jnp.broadcast_to(column(cnt_ref[...]), (nb, LANES))
-    amask[...] = jnp.where((order // TILE).astype(F32) == row_column, 1.0, 0.0)
+    amask[...] = jnp.where(tile_of.astype(F32) == row_column, 1.0, 0.0)
+    lane_tile = iota((nb, LANES), 1).astype(F32)
+    select[0:nb, :] = onehot(rowtile[...] == lane_tile)
+    select[nb : 2 * nb, :] = onehot(coltile[...] == lane_tile)
 
     row_k = iota((PAD, n), 0)
     stiffness = jnp.ones((PAD, n), F32)
@@ -270,50 +277,37 @@
         stiffness = jnp.where(row_k == k, pen_ref[k], stiffness)
 
     def spread_gains(phase):
-        held = jnp.concatenate(
-            [
-                jnp.concatenate([gbuf[phase, b, d, c] for b in range(nbl)], axis=1)
-                for d in range(ndir)
-                for c in range(2)
-            ],
-            axis=0,
-        )
-        first = held.astype(BF16)
-        rest = held - first.astype(F32)
-        second = rest.astype(BF16)
-        third = (rest - second.astype(F32)).astype(BF16)
-        pieces = jnp.concatenate([first, second, third], axis=0)
-        found = lax.dot_general(
-            pieces, dmat[...], (((1,), (1,)), ((), ())), preferred_element_type=F32
-        )
-        count = held.shape[0]
-        natscr[...] = found[0:count] + found[count : 2 * count] + found[2 * count : 3 * count]
-
-        def one(index, carry):
-            group = index // kl
-            row = group * PAD + lax.rem(index, kl)
-            values = natscr[pl.ds(row, 1), :]
-            by_row = jnp.zeros((nb, LANES), F32)
-            by_col = jnp.zeros((nb, LANES), F32)
-            for t in range(ntile):
-                tile = values[:, t * LANES : (t + 1) * LANES]
-                by_row = jnp.where(rowtile[...] == float(t), tile, by_row)
-                by_col = jnp.where(coltile[...] == float(t), tile, by_col)
-            at = pl.ds(pl.multiple_of(index * nb, nb), nb)
-            low_lanes = iota((nb, LANES), 1) < TILE
-            for gains_of, split in ((by_row, rsplit), (by_col, csplit)):
-                first, rest = two_pieces(gains_of)
-                rest = gains_of - first.astype(F32)
-                second, third = two_pieces(rest)
-                split[at, 0:LANES] = jnp.where(
-                    low_lanes, first.astype(F32), second.astype(F32)
-                ).astype(BF16)
-                split[at, LANES : 2 * LANES] = third
-            return carry
-
-        lax.fori_loop(0, 2 * kall, one, 0)
-        rowexp[...] = jnp.dot(rsplit[...], rowmat[...], preferred_element_type=F32)
-        colexp[...] = jnp.dot(csplit[...], colmat[...], preferred_element_type=F32)
+        highs, lows = [], []
+        for d in range(ndir):
+            for c in range(2):
+                held = jnp.concatenate([gbuf[phase, b, d, c] for b in range(nbl)], axis=1)
+                first = held.astype(BF16).astype(F32)
+                second = held - first
+                for k in range(kl):
+                    highs.append(first[k : k + 1, :] * tilemask[...])
+                    lows.append(second[k : k + 1, :] * tilemask[...])
+        pieces = jnp.concatenate(
+            [jnp.concatenate(highs, axis=0), jnp.concatenate(lows, axis=0)], axis=1
+        ).astype(BF16)
+        natural = lax.dot_general(
+            pieces, inmat[...], (((1,), (1,)), ((), ())), preferred_element_type=F32
+        )
+        by_tile = jnp.concatenate(
+            [natural[i * PAD : (i + 1) * PAD, :] for i in range(2 * kall)], axis=1
+        )
+        by_tile = jnp.concatenate([by_tile, jnp.zeros_like(by_tile)], axis=0).astype(BF16)
+        chosen = jnp.dot(
+            select[:, 0 : 2 * PAD], by_tile, preferred_element_type=F32
+        ).astype(BF16)
+        for first, table, target in ((0, rowmat, rowexp), (nb, colmat, colexp)):
+            stacked = jnp.concatenate(
+                [
+                    chosen[first : first + nb, i * LANES : (i + 1) * LANES]
+                    for i in range(2 * kall)
+                ],
+                axis=0,
+            )
+            target[...] = jnp.dot(stacked, table[...], preferred_element_type=F32)
 
     def permute_half(d):
         def step(g, carry):
@@ -346,7 +340,7 @@
                 return pl.ds(pl.multiple_of(index * nb + part * PAD, PAD), PAD)
 
             lane = iota((PAD, LANES), 1)
-            row = md * rows_half + g * rows_group + lane // per_row
+            row = md * rows_half + g * rows_group + lax.shift_right_logical(lane, shift_of(per_row))
             same = rowtile[blocks, :] == coltile[blocks, :]
             totals = [jnp.zeros((PAD, LANES), F32)] * (3 * kall)
             for v in range(FOLD):
@@ -470,6 +464,11 @@
         finish(copies)
 
 
+def hand_over(gain_ref, dual_ref, gout_ref, dout_ref):
+    gout_ref[...] = gain_ref[...]
+    dout_ref[...] = dual_ref[...]
+
+
 def on_device(
     nchan, nbl, ndir,
     visibility, coherency, gain_start, dual_start, penalty, tile_pairs, valid_counts, station_order,
@@ -480,7 +479,6 @@
     stations = nbl * n
     half = TILE * TILE // ndir
     kall = ndir * kl
-    ntile = stations // TILE
     nown = nbl * ndir
     vmem = pl.BlockSpec(memory_space=pltpu.VMEM)
     smem = pl.BlockSpec(memory_space=pltpu.SMEM)
@@ -508,16 +506,15 @@
             pltpu.VMEM((ITERS, nbl, ndir, 3, PAD, n), F32),
             pltpu.VMEM((ITERS, nbl, ndir, 3, PAD, n), F32),
             pltpu.VMEM((2, PAD, n), F32),
-            pltpu.VMEM((ndir * 2 * PAD, ntile * LANES), F32),
-            pltpu.VMEM((ntile * LANES, stations), BF16),
             pltpu.VMEM((GROUP, GROUP), BF16),
-            pltpu.VMEM((2 * LANES, ngroup * LANES), BF16),
-            pltpu.VMEM((2 * LANES, GROUP), BF16),
+            pltpu.VMEM((LANES, ngroup * LANES), BF16),
+            pltpu.VMEM((LANES, GROUP), BF16),
             pltpu.VMEM((2 * ngroup * LANES, LANES), BF16),
             pltpu.VMEM((2 * LANES, stations), BF16),
             pltpu.VMEM((nb, stations), F32),
-            pltpu.VMEM((2 * kall * nb, 2 * LANES), BF16),
-            pltpu.VMEM((2 * kall * nb, 2 * LANES), BF16),
+            pltpu.VMEM((PAD, stations), F32),
+            pltpu.VMEM((LANES, 2 * stations), BF16),
+            pltpu.VMEM((2 * nb, LANES), BF16),
             pltpu.VMEM((2 * kall * nb, ngroup * LANES), F32),
             pltpu.VMEM((2 * kall * nb, GROUP), F32),
             pltpu.VMEM((3 * kall * nb, ngroup * LANES), F32),
@@ -547,6 +544,9 @@
         valid_counts.reshape(1, nb),
         station_order.reshape(1, stations),
     )
+    gain, dual = pl.pallas_call(
+        hand_over, out_shape=(out, out), in_specs=[vmem, vmem], out_specs=(vmem, vmem)
+    )(gain, dual)
     return jnp.transpose(gain, (0, 2, 1, 3)), jnp.transpose(dual, (0, 2, 1, 3))
 
 

time: 41.2 us -> 37.2 us (0.903)
  local copies, waits for them, and re-layouts: 2.6 us -> 0 us
  Pallas kernels: 37.6 us -> 36.3 us
    pallas_call x1, Pallas kernels: 37.6 us -> 35 us  [on_device(): pl.pallas_call(functools.partial(kernel, nchan, nbl, ndir, poly_coefficie...]
    unnamed x2 -> x0, local copies, waits for them, and re-layouts: 2.6 us -> none
    pallas_call x0 -> x1, Pallas kernels: none -> 1.33 us  [on_device(): pl.pallas_call(hand_over, out_shape=(out, out), in_specs=[vmem, vmem], ou...]
where the time goes in v2:
time: 37.2 us; the launch traced here: 36.9 us
  Pallas kernels  36.3 us (98%)
  between operations  0.64 us (2%)
    pallas_call x1, Pallas kernels, on_device(): pl.pallas_call(functools.partial(kernel, nchan, nbl, ndir, poly_coefficie...  35 us
    pallas_call x1, Pallas kernels, on_device(): pl.pallas_call(hand_over, out_shape=(out, out), in_specs=[vmem, vmem], ou...  1.33 us

profile of v2, /device:TPU:0, one launch (start us, length us, event | category | flops | bytes accessed | tf_op | source)
XLA Modules:
  0.0 36.9 jit_solution(7178236278566517827)
XLA Ops:
  0.6 35.0 %shard_map.95 = (f32[2,5,1,256]{3,2,1,0:T(1,128)}, f32[2,5,1,256]{3,2,1,0:T(1,128)}) custom-call(bf16[2,1,5,32,4096]{4,3,2,1,0:T(8,128)(2,1)} %coh_hbm.1, bf16[2,1,32,4096]{3,2,1,0:T(8,128)(2,1)} %vis_hbm.1, f32[2,5,1,256]{3,2,1,0:T(1,128)} %bitcast.7, f32[2,5,1,256]{3,2,1,0:T(1,128)} %bitcast.8, f32[5]{0:T(128)} %pen_ref.1, s32[2,32]{1,0:T(2,128)} %bitcast.10, ...), custom_call_target="tpu_custom_call" | custom-call | tf_op jit(solution)/shard_map/pallas_call | solution.py:489
  35.6 1.3 %shard_map.96 = (f32[2,5,1,256]{3,2,1,0:T(1,128)}, f32[2,5,1,256]{3,2,1,0:T(1,128)}) custom-call(f32[2,5,1,256]{3,2,1,0:T(1,128)} %get-tuple-element.6.gain_ref, f32[2,5,1,256]{3,2,1,0:T(1,128)} %get-tuple-element.7.dual_ref), custom_call_target="tpu_custom_call" | custom-call | tf_op jit(solution)/shard_map/pallas_call | solution.py:547

commit v3 on v2

--- a/solution.py
+++ b/solution.py
@@ -66,7 +66,7 @@
     gout_ref, dout_ref,
     cohv, visv, cohp, visp, gain_ref, dual_ref, pairs_ref, cnt_ref, ord_ref,
     gbuf, cbuf, psend, prec, dualp, perm, rowmat, colmat, rmat, imat, amask,
-    tilemask, inmat, select, rowexp, colexp, tbuf, rowtile, coltile, limit,
+    tilemask, inmat, select, rowexp, colexp, cross, tbuf, rowtile, coltile, limit,
     lsem, hsend, hrecv, gsend, grecv, csend, crecv, psems, precv,
 ):
     chan = lax.axis_index("chan")
@@ -174,10 +174,10 @@
                 device_id_type=MESH,
             )
             copy = pltpu.make_async_remote_copy(
-                dst_ref=target.at[phase, mb, md], recv_sem=recv_sem.at[phase, mine], **common
+                dst_ref=target.at[phase, mb, md, :, 0:kl, :], recv_sem=recv_sem.at[phase, mine], **common
             )
             arrival = pltpu.make_async_remote_copy(
-                dst_ref=target.at[phase, sb, sd],
+                dst_ref=target.at[phase, sb, sd, :, 0:kl, :],
                 recv_sem=recv_sem.at[phase, sb * ndir + sd],
                 **common,
             )
@@ -185,10 +185,14 @@
         return made
 
     def gain_copies(phase):
-        return group_copies(lambda pb, pd: gbuf.at[phase, mb, md], gbuf, gsend, grecv, phase)
+        return group_copies(
+            lambda pb, pd: gbuf.at[phase, mb, md, :, 0:kl, :], gbuf, gsend, grecv, phase
+        )
 
     def term_copies(phase):
-        return group_copies(lambda pb, pd: psend.at[phase, pb, pd], prec, psems, precv, phase)
+        return group_copies(
+            lambda pb, pd: psend.at[phase, pb, pd, :, 0:kl, :], prec, psems, precv, phase
+        )
 
     def chan_copies(phase):
         made = []
@@ -196,16 +200,16 @@
             peer = chan_peer(offset)
             source = chan_peer(nchan - offset)
             common = dict(
-                src_ref=cbuf.at[phase, chan],
+                src_ref=cbuf.at[phase, chan, :, 0:kl, :],
                 send_sem=csend.at[phase, offset],
                 device_id={"chan": peer},
                 device_id_type=MESH,
             )
             copy = pltpu.make_async_remote_copy(
-                dst_ref=cbuf.at[phase, chan], recv_sem=crecv.at[phase, chan], **common
+                dst_ref=cbuf.at[phase, chan, :, 0:kl, :], recv_sem=crecv.at[phase, chan], **common
             )
             arrival = pltpu.make_async_remote_copy(
-                dst_ref=cbuf.at[phase, source], recv_sem=crecv.at[phase, source], **common
+                dst_ref=cbuf.at[phase, source, :, 0:kl, :], recv_sem=crecv.at[phase, source], **common
             )
             made.append((copy, arrival))
         return made
@@ -309,12 +313,28 @@
             )
             target[...] = jnp.dot(stacked, table[...], preferred_element_type=F32)
 
+    def valid_slots(g):
+        lane = iota((nb, GROUP), 1)
+        in_lane = jnp.bitwise_and(lane, LANES - 1)
+        row = md * rows_half + g * rows_group + lax.shift_right_logical(in_lane, shift_of(per_row))
+        col = lax.shift_right_logical(lane, shift_of(LANES)) * per_row + jnp.bitwise_and(
+            lane, per_row - 1
+        )
+
+        def across(table):
+            return jnp.concatenate([table[...]] * FOLD, axis=1)
+
+        inside = (row * TILE + col).astype(F32) < across(limit)
+        same = across(rowtile) == across(coltile)
+        return jnp.where(inside & jnp.logical_not(same & (row == col)), 1.0, 0.0)
+
     def permute_half(d):
         def step(g, carry):
             lanes = pl.ds(pl.multiple_of(g * GROUP, GROUP), GROUP)
             source = cohv[d, :, :, :, lanes].reshape(2 * kl * nb, GROUP)
             moved = jnp.dot(source, perm[...], preferred_element_type=F32)
-            cohp[d, :, :, :, lanes] = moved.reshape(2, kl, nb, GROUP)
+            moved = moved.reshape(2, kl, nb, GROUP)
+            cohp[d, :, :, :, lanes] = moved * valid_slots(g)[None, None]
             return carry
 
         lax.fori_loop(0, ngroup, step, 0)
@@ -339,16 +359,12 @@
             def at(index):
                 return pl.ds(pl.multiple_of(index * nb + part * PAD, PAD), PAD)
 
-            lane = iota((PAD, LANES), 1)
-            row = md * rows_half + g * rows_group + lax.shift_right_logical(lane, shift_of(per_row))
-            same = rowtile[blocks, :] == coltile[blocks, :]
-            totals = [jnp.zeros((PAD, LANES), F32)] * (3 * kall)
+            residuals = []
             for v in range(FOLD):
                 here = pl.ds(pl.multiple_of(g * GROUP + v * LANES, LANES), LANES)
                 cols = slice(v * LANES, (v + 1) * LANES)
                 model_r = jnp.zeros((PAD, LANES), F32)
                 model_i = jnp.zeros((PAD, LANES), F32)
-                cross = []
                 for d in range(ndir):
                     for k in range(kl):
                         re, im = d * 2 * kl + k, d * 2 * kl + kl + k
@@ -357,45 +373,51 @@
                         col_r, col_i = colexp[at(re), cols], colexp[at(im), cols]
                         cr = coh_r * col_r + coh_i * col_i
                         ci = coh_i * col_r - coh_r * col_i
+                        cross[d * kl + k, 0, v] = cr
+                        cross[d * kl + k, 1, v] = ci
                         row_r, row_i = rowexp[at(re), lanes], rowexp[at(im), lanes]
                         model_r = model_r + (row_r * cr - row_i * ci)
                         model_i = model_i + (row_r * ci + row_i * cr)
-                        cross.append((cr, ci))
-                col = v * per_row + jnp.bitwise_and(lane, per_row - 1)
-                inside = (row * TILE + col).astype(F32) < limit[blocks, :]
-                valid = jnp.where(inside & jnp.logical_not(same & (row == col)), 1.0, 0.0)
-                res_r = valid * (visp[0, blocks, here] - model_r)
-                res_i = valid * (visp[1, blocks, here] - model_i)
-                for index, (cr, ci) in enumerate(cross):
-                    terms = (
+                res_r = visp[0, blocks, here] - model_r
+                res_i = visp[1, blocks, here] - model_i
+                residuals.append((res_r, res_i))
+            for index in range(kall):
+                numer_r = numer_i = weight = None
+                for v, (res_r, res_i) in enumerate(residuals):
+                    cr, ci = cross[index, 0, v], cross[index, 1, v]
+                    parts = (
                         res_r * cr + res_i * ci,
                         res_i * cr - res_r * ci,
-                        valid * (cr * cr + ci * ci),
+                        cr * cr + ci * ci,
                     )
-                    for q, term in enumerate(terms):
-                        totals[q * kall + index] = totals[q * kall + index] + term
-            for index, total in enumerate(totals):
-                tbuf[at(index), lanes] = total
+                    if numer_r is None:
+                        numer_r, numer_i, weight = parts
+                    else:
+                        numer_r = numer_r + parts[0]
+                        numer_i = numer_i + parts[1]
+                        weight = weight + parts[2]
+                tbuf[at(index), lanes] = numer_r
+                tbuf[at(kall + index), lanes] = numer_i
+                tbuf[at(2 * kall + index), lanes] = weight
             return carry
 
         lax.fori_loop(0, ngroup * (nb // PAD), tile_step, 0)
 
+        high, low = two_pieces(tbuf[...])
+        by_block = jnp.dot(
+            jnp.concatenate([high, low], axis=1), rmat[...], preferred_element_type=F32
+        )
+        high, low = two_pieces(by_block)
+        placed = jnp.dot(
+            jnp.concatenate([high, low], axis=1), imat[...], preferred_element_type=F32
+        )
+        kept = placed.reshape(3 * kall, nb, stations) * amask[...][None]
+        summed = jnp.sum(kept, axis=1)
         for q in range(3):
-            high, low = two_pieces(tbuf[q * kall * nb : (q + 1) * kall * nb, :])
-            by_block = jnp.dot(
-                jnp.concatenate([high, low], axis=1), rmat[...], preferred_element_type=F32
-            )
-            high, low = two_pieces(by_block)
-            placed = jnp.dot(
-                jnp.concatenate([high, low], axis=1), imat[...], preferred_element_type=F32
-            )
-            kept = placed.reshape(kall, nb, stations) * amask[...][None]
-            summed = jnp.sum(kept, axis=1)
             for d in range(ndir):
+                at = (q * ndir + d) * kl
                 for b in range(nbl):
-                    psend[phase, b, d, q, 0:kl, :] = summed[
-                        d * kl : (d + 1) * kl, b * n : (b + 1) * n
-                    ]
+                    psend[phase, b, d, q, 0:kl, :] = summed[at : at + kl, b * n : (b + 1) * n]
 
     mine_basis = basis_at(chan, nchan, coefficients)
 
@@ -517,6 +539,7 @@
             pltpu.VMEM((2 * nb, LANES), BF16),
             pltpu.VMEM((2 * kall * nb, ngroup * LANES), F32),
             pltpu.VMEM((2 * kall * nb, GROUP), F32),
+            pltpu.VMEM((kall, 2, FOLD, PAD, LANES), F32),
             pltpu.VMEM((3 * kall * nb, ngroup * LANES), F32),
             pltpu.VMEM((nb, LANES), F32),
             pltpu.VMEM((nb, LANES), F32),

time: 37.2 us -> 35.3 us (0.949)
  Pallas kernels: 36.3 us -> 34.4 us
    pallas_call x1, Pallas kernels: 35 us -> 33.1 us  [on_device(): pl.pallas_call(functools.partial(kernel, nchan, nbl, ndir, poly_coefficie...]
where the time goes in v3:
time: 35.3 us; the launch traced here: 35 us
  Pallas kernels  34.4 us (97%)
  between operations  0.64 us (2%)
    pallas_call x1, Pallas kernels, on_device(): pl.pallas_call(functools.partial(kernel, nchan, nbl, ndir, poly_coefficie...  33.1 us
    pallas_call x1, Pallas kernels, on_device(): pl.pallas_call(hand_over, out_shape=(out, out), in_specs=[vmem, vmem], ou...  1.33 us

profile of v3, /device:TPU:0, one launch (start us, length us, event | category | flops | bytes accessed | tf_op | source)
XLA Modules:
  0.0 35.0 jit_solution(9980032365968601562)
XLA Ops:
  0.6 33.1 %shard_map.95 = (f32[2,5,1,256]{3,2,1,0:T(1,128)}, f32[2,5,1,256]{3,2,1,0:T(1,128)}) custom-call(bf16[2,1,5,32,4096]{4,3,2,1,0:T(8,128)(2,1)} %coh_hbm.1, bf16[2,1,32,4096]{3,2,1,0:T(8,128)(2,1)} %vis_hbm.1, f32[2,5,1,256]{3,2,1,0:T(1,128)} %bitcast.7, f32[2,5,1,256]{3,2,1,0:T(1,128)} %bitcast.8, f32[5]{0:T(128)} %pen_ref.1, s32[2,32]{1,0:T(2,128)} %bitcast.10, ...), custom_call_target="tpu_custom_call" | custom-call | tf_op jit(solution)/shard_map/pallas_call | solution.py:511
  33.7 1.3 %shard_map.96 = (f32[2,5,1,256]{3,2,1,0:T(1,128)}, f32[2,5,1,256]{3,2,1,0:T(1,128)}) custom-call(f32[2,5,1,256]{3,2,1,0:T(1,128)} %get-tuple-element.6.gain_ref, f32[2,5,1,256]{3,2,1,0:T(1,128)} %get-tuple-element.7.dual_ref), custom_call_target="tpu_custom_call" | custom-call | tf_op jit(solution)/shard_map/pallas_call | solution.py:570

commit v4 on v3

--- a/solution.py
+++ b/solution.py
@@ -97,6 +97,15 @@
     def own_half():
         return pl.ds(pl.multiple_of(md * half, half), half)
 
+    barrier = pltpu.get_barrier_semaphore()
+    for offset in range(1, nown):
+        pb, pd = group_peer(offset)
+        pl.semaphore_signal(barrier, inc=1, device_id={"bl": pb, "dir": pd}, device_id_type=MESH)
+    for offset in range(1, nchan):
+        pl.semaphore_signal(
+            barrier, inc=1, device_id={"chan": chan_peer(offset)}, device_id_type=MESH
+        )
+
     small = [
         pltpu.make_async_copy(source, target, lsem.at[2 + index])
         for index, (source, target) in enumerate(
@@ -116,19 +125,9 @@
     for copy in small + local:
         copy.start()
 
-    barrier = pltpu.get_barrier_semaphore()
-    for offset in range(1, nown):
-        pb, pd = group_peer(offset)
-        pl.semaphore_signal(barrier, inc=1, device_id={"bl": pb, "dir": pd}, device_id_type=MESH)
-    for offset in range(1, nchan):
-        pl.semaphore_signal(
-            barrier, inc=1, device_id={"chan": chan_peer(offset)}, device_id_type=MESH
-        )
-
     gbuf[0, mb, md] = jnp.zeros((2, PAD, n), F32)
     dualp[...] = jnp.zeros((2, PAD, n), F32)
-    psend[...] = jnp.zeros(psend.shape, F32)
-    for copy in small:
+    for copy in small[:2]:
         copy.wait()
     for c in range(2):
         for k in range(kl):
@@ -234,6 +233,9 @@
     start(sums)
     everything += [gains, halves, sums]
 
+    psend[...] = jnp.zeros(psend.shape, F32)
+    for copy in small[2:]:
+        copy.wait()
     order = ord_ref[...]
     within = jnp.bitwise_and(order, TILE - 1)
     tile_of = lax.shift_right_logical(order, shift_of(TILE))
@@ -337,7 +339,7 @@
             cohp[d, :, :, :, lanes] = moved * valid_slots(g)[None, None]
             return carry
 
-        lax.fori_loop(0, ngroup, step, 0)
+        lax.fori_loop(0, ngroup, step, 0, unroll=True)
 
     def permute_vis():
         def step(g, carry):
@@ -347,7 +349,7 @@
             visp[:, :, lanes] = moved.reshape(2, nb, GROUP)
             return carry
 
-        lax.fori_loop(0, ngroup, step, 0)
+        lax.fori_loop(0, ngroup, step, 0, unroll=True)
 
     def station_terms(phase):
         def tile_step(step, carry):
@@ -401,7 +403,7 @@
                 tbuf[at(2 * kall + index), lanes] = weight
             return carry
 
-        lax.fori_loop(0, ngroup * (nb // PAD), tile_step, 0)
+        lax.fori_loop(0, ngroup * (nb // PAD), tile_step, 0, unroll=4)
 
         high, low = two_pieces(tbuf[...])
         by_block = jnp.dot(
@@ -436,12 +438,11 @@
                 copy.wait()
             permute_half(md)
             permute_vis()
-        arrive(gains)
-        spread_gains(iteration)
-        if iteration == 0:
             arrive(halves)
             for offset in range(1, ndir):
                 permute_half(lax.rem(md + offset, ndir))
+        arrive(gains)
+        spread_gains(iteration)
         station_terms(iteration)
         moved = term_copies(iteration)
         start(moved)
@@ -464,12 +465,12 @@
                 for c in range(2)
             ]
         )
-        cbuf[iteration + 1, chan] = gain_now + dual_now
         if iteration + 1 < ITERS:
             gbuf[iteration + 1, mb, md] = gain_now
             gains = gain_copies(iteration + 1)
             start(gains)
             everything.append(gains)
+        cbuf[iteration + 1, chan] = gain_now + dual_now
         sums = chan_copies(iteration + 1)
         start(sums)
         everything.append(sums)

time: 35.3 us -> 34.3 us (0.972)
  Pallas kernels: 34.4 us -> 33.4 us
    pallas_call x1, Pallas kernels: 33.1 us -> 32 us  [on_device(): pl.pallas_call(functools.partial(kernel, nchan, nbl, ndir, poly_coefficie...]
where the time goes in v4:
time: 34.3 us; the launch traced here: 34 us
  Pallas kernels  33.4 us (97%)
  between operations  0.64 us (2%)
    pallas_call x1, Pallas kernels, on_device(): pl.pallas_call(functools.partial(kernel, nchan, nbl, ndir, poly_coefficie...  32 us
    pallas_call x1, Pallas kernels, on_device(): pl.pallas_call(hand_over, out_shape=(out, out), in_specs=[vmem, vmem], ou...  1.33 us

profile of v4, /device:TPU:0, one launch (start us, length us, event | category | flops | bytes accessed | tf_op | source)
XLA Modules:
  0.0 34.0 jit_solution(6830751846156107077)
XLA Ops:
  0.6 32.0 %shard_map.95 = (f32[2,5,1,256]{3,2,1,0:T(1,128)}, f32[2,5,1,256]{3,2,1,0:T(1,128)}) custom-call(bf16[2,1,5,32,4096]{4,3,2,1,0:T(8,128)(2,1)} %coh_hbm.1, bf16[2,1,32,4096]{3,2,1,0:T(8,128)(2,1)} %vis_hbm.1, f32[2,5,1,256]{3,2,1,0:T(1,128)} %bitcast.7, f32[2,5,1,256]{3,2,1,0:T(1,128)} %bitcast.8, f32[5]{0:T(128)} %pen_ref.1, s32[2,32]{1,0:T(2,128)} %bitcast.10, ...), custom_call_target="tpu_custom_call" | custom-call | tf_op jit(solution)/shard_map/pallas_call | solution.py:512
  32.7 1.3 %shard_map.96 = (f32[2,5,1,256]{3,2,1,0:T(1,128)}, f32[2,5,1,256]{3,2,1,0:T(1,128)}) custom-call(f32[2,5,1,256]{3,2,1,0:T(1,128)} %get-tuple-element.6.gain_ref, f32[2,5,1,256]{3,2,1,0:T(1,128)} %get-tuple-element.7.dual_ref), custom_call_target="tpu_custom_call" | custom-call | tf_op jit(solution)/shard_map/pallas_call | solution.py:571
